TPU v7x, 256 devices: a whole 4x4x8 slice. The times are simulated.
256 devices in a mesh: tile: 32 (over y, z_lo, core), freq: 8 (over z_hi, x).
Axes of the slice: x: 4, y: 4, z: 8 (z_hi: 2, z_lo: 4; z = z_hi * 4 + z_lo), core: 2. Of those that a mesh axis runs over, the one named last changes fastest.
Arguments:
- leaf_maps: bfloat16 [8, 65536, 2048], P('freq', 'tile'), as said below
- wave_index: int32 [8], P('freq'), may hold values from 0 to 7, as said below
- medium: bfloat16 [16384, 512], P('tile'), may hold values from 0.5 to 2
- source: bfloat16 [8, 16384, 512], P('freq', 'tile'), may hold values from -6 to 6
- state_field: bfloat16 [8, 16384, 512], P('freq', 'tile'), may hold values from -6 to 6
- adjoint_field: bfloat16 [8, 16384, 512], P('freq', 'tile'), may hold values from -6 to 6
- receivers: int32 [8, 8192], P('freq', 'tile'), may hold values from 0 to 262143
- recorded: bfloat16 [8, 8192], P('freq', 'tile'), may hold values from -180 to 180
Outputs:
- merged_maps: bfloat16 [8, 16384, 2048], P('freq', 'tile')
- medium_gradient: float32 [16384, 512], P(('tile', 'freq'))
Inputs may be any that keep to these rules, and one draw needn't show every extreme that they name: leaf_maps: every leaf box map is exactly symmetric and positive definite. wave_index: the first eight frequencies (all of them if fewer) have distinct values.
All inputs are finite; a program needn't handle non-finite values.
Results may differ from a plain program's by a relative error of at most 0.0082.
Values may be sent and summed in bfloat16 or wider, within the bound.
No kernel may reach another device: no remote copies, remote signals or barrier semaphores. Data moves between devices by JAX's collectives and lax.ppermute only.
A program may use at most 192 MiB of HBM per device.

v0:
```python
import jax
import jax.numpy as jnp
from jax import lax
from jax.sharding import PartitionSpec as P


def from_partner(block, axis, distance):
    count = lax.axis_size(axis)
    route = []
    for low in range(count):
        high = low | 1 << distance
        if high != low and high < count:
            route += [(low, high), (high, low)]
    return lax.ppermute(block, axis, route)


def extended(block, sides, width):
    for axis, dim in sides:
        count = lax.axis_size(axis)
        forward = [(i, i + 1) for i in range(count - 1)]
        backward = [(target, source) for source, target in forward]
        low = lax.ppermute(
            lax.slice_in_dim(block, block.shape[dim] - width, None, axis=dim), axis, forward
        )
        high = lax.ppermute(lax.slice_in_dim(block, 0, width, axis=dim), axis, backward)
        block = jnp.concatenate([low, block, high], axis=dim)
    return block


def ordered(flag, own_part, partner, axis_number):
    return jnp.where(
        flag == 0,
        jnp.concatenate([own_part, partner], axis=axis_number),
        jnp.concatenate([partner, own_part], axis=axis_number),
    )


def placed(flag, own_block, total_width):
    zero_block = jnp.zeros((own_block.shape[0], total_width - own_block.shape[1]), jnp.float32)
    return ordered(flag, own_block, zero_block, 1)


def triangular(factor, right_side):
    return jax.scipy.linalg.solve_triangular(factor, right_side, lower=True)


def level_one(leaf_map, low_bit):
    half_size = leaf_map.shape[0] // 2
    own_inner = leaf_map[half_size:, half_size:]
    own_coupling = leaf_map[:half_size, half_size:].T.astype(jnp.float32)
    partner_inner = from_partner(own_inner, "tile", 0)
    schur = own_inner.astype(jnp.float32) + partner_inner.astype(jnp.float32)
    factor = jnp.linalg.cholesky(schur)
    solved_own = triangular(factor, own_coupling).astype(jnp.bfloat16)
    solved_partner = from_partner(solved_own, "tile", 0)
    solved_all = ordered(low_bit, solved_own, solved_partner, 1)
    coupling = lax.dot_general(
        solved_own, solved_all, (((0,), (0,)), ((), ())), preferred_element_type=jnp.float32
    )
    own_block = leaf_map[:half_size, :half_size].astype(jnp.float32)
    return (placed(low_bit, own_block, 2 * half_size) - coupling).astype(jnp.bfloat16)


def level_two(own_rows, low_bit, high_bit):
    half_size = own_rows.shape[0]
    quarter = half_size // 2
    inner_cols = jnp.concatenate(
        [own_rows[:, quarter:half_size], own_rows[:, half_size + quarter :]], axis=1
    )
    outer_cols = jnp.concatenate(
        [own_rows[:, :quarter], own_rows[:, half_size : half_size + quarter]], axis=1
    )
    inner_piece = inner_cols[quarter:]
    sibling_piece = from_partner(inner_piece, "tile", 1)
    half_sum = inner_piece.astype(jnp.float32) + sibling_piece.astype(jnp.float32)
    partner_sum = from_partner(half_sum, "tile", 0)
    schur = ordered(low_bit, half_sum, partner_sum, 0)
    factor = jnp.linalg.cholesky(schur)
    solved_own = triangular(factor, inner_cols[:quarter].T.astype(jnp.float32)).astype(jnp.bfloat16)
    solved_partner = from_partner(solved_own, "tile", 0)
    solved_pair = ordered(low_bit, solved_own, solved_partner, 1)
    solved_sibling = from_partner(solved_pair, "tile", 1)
    solved_all = ordered(high_bit, solved_pair, solved_sibling, 1)
    coupling = lax.dot_general(
        solved_own, solved_all, (((0,), (0,)), ((), ())), preferred_element_type=jnp.float32
    )
    own_block = outer_cols[:quarter].astype(jnp.float32)
    return (placed(high_bit, own_block, 2 * half_size) - coupling).astype(jnp.bfloat16)


def stencil(padded, field):
    edges = (
        padded[..., 2:, 1:-1]
        + padded[..., :-2, 1:-1]
        + padded[..., 1:-1, 2:]
        + padded[..., 1:-1, :-2]
    )
    corners = (
        padded[..., 2:, 2:] + padded[..., 2:, :-2] + padded[..., :-2, 2:] + padded[..., :-2, :-2]
    )
    return (4.0 * edges + corners - 20.0 * field) / 6.0


def body(leaf_maps, wave_index, medium, source, state_field, adjoint_field, receivers, recorded):
    tile_index = lax.axis_index("tile")
    low_bit = jnp.bitwise_and(tile_index, 1)
    high_bit = jnp.bitwise_and(jnp.right_shift(tile_index, 1), 1)
    stacked = jnp.stack([state_field, adjoint_field])
    rimmed = extended(stacked, (("tile", 2),), 1)
    rimmed = jnp.pad(rimmed.astype(jnp.float32), ((0, 0), (0, 0), (0, 0), (1, 1)))
    pair_rows = level_one(leaf_maps[0], low_bit)
    merged_list = [level_two(pair_rows, low_bit, high_bit)]
    merged_maps = jnp.stack(merged_list)
    fields = stacked.astype(jnp.float32)
    kappa = 0.2 * (1.0 + wave_index.astype(jnp.float32))
    kappa_sq = (kappa * kappa)[:, None, None]
    medium_full = medium.astype(jnp.float32)[None]
    applied = stencil(rimmed, fields) + kappa_sq[None] * medium_full[None] * fields
    state_full = fields[0]
    adjoint_full = fields[1]
    state_residual = source.astype(jnp.float32) - applied[0]
    box_cells = state_full.shape[1] * state_full.shape[2]
    flat_state = state_full.reshape(state_full.shape[0], box_cells)
    misfit = jnp.take_along_axis(flat_state, receivers, axis=1) - recorded.astype(jnp.float32)
    freq_rows = jnp.broadcast_to(
        jnp.arange(receivers.shape[0], dtype=jnp.int32)[:, None], receivers.shape
    )
    adjoint_source = (
        jnp.zeros(flat_state.shape, jnp.float32)
        .at[freq_rows, receivers]
        .add(misfit)
        .reshape(state_full.shape)
    )
    adjoint_residual = adjoint_source - applied[1]
    gradient_term = -jnp.sum(
        kappa_sq * (state_full * state_residual + adjoint_full * adjoint_residual), axis=0
    )
    share_rows = gradient_term.shape[0] // lax.axis_size("freq")
    total = lax.psum(gradient_term, "freq")
    medium_gradient = lax.dynamic_slice_in_dim(
        total, lax.axis_index("freq") * share_rows, share_rows, 0
    )
    return (merged_maps, medium_gradient)


def solution(mesh):
    placed = (
        P("freq", "tile", None),
        P("freq"),
        P("tile", None),
        P("freq", "tile", None),
        P("freq", "tile", None),
        P("freq", "tile", None),
        P("freq", "tile"),
        P("freq", "tile"),
    )
    return jax.shard_map(
        body,
        mesh=mesh,
        in_specs=placed,
        out_specs=(P("freq", "tile", None), P(("tile", "freq"), None)),
        check_vma=False,
    )
```

profile of v0, /device:TPU:8, one launch (start us, length us, event | category | flops | bytes accessed | tf_op | source)
XLA Modules:
  0.0 1019.6 jit_solution(1663486768981271315)
XLA Ops:
  7.2 12.3 %copy.32 = bf16[1,2048,2048]{1,2,0:T(8,128)(2,1)} copy(bf16[1,2048,2048]{2,1,0:T(8,128)(2,1)} %param.9) | data formatting | bytes 16777216 | tf_op args[0]
  47.9 11.7 %cholesky.619 = f32[128,128]{1,0:T(8,128)S(1)} custom-call(f32[128,128]{1,0:T(8,128)S(1)} %cholesky.911), custom_call_target="Cholesky" | custom-call | tf_op jit(solution)/shard_map/jit(cholesky)/cholesky | solution.py:53
  59.6 9.8 custom-call.61
  75.9 12.2 %cholesky.638 = f32[128,128]{1,0:T(8,128)S(1)} custom-call(f32[128,128]{1,0:T(8,128)S(1)} %cholesky.915), custom_call_target="Cholesky" | custom-call | tf_op jit(solution)/shard_map/jit(cholesky)/cholesky | solution.py:53
  101.9 11.7 %cholesky.659 = f32[128,128]{1,0:T(8,128)S(1)} custom-call(f32[128,128]{1,0:T(8,128)S(1)} %cholesky.920), custom_call_target="Cholesky" | custom-call | tf_op jit(solution)/shard_map/jit(cholesky)/cholesky | solution.py:53
  128.2 11.9 %cholesky.678 = f32[128,128]{1,0:T(8,128)S(1)} custom-call(f32[128,128]{1,0:T(8,128)S(1)} %cholesky.925), custom_call_target="Cholesky" | custom-call | tf_op jit(solution)/shard_map/jit(cholesky)/cholesky | solution.py:53
  154.7 11.7 %cholesky.697 = f32[128,128]{1,0:T(8,128)S(1)} custom-call(f32[128,128]{1,0:T(8,128)S(1)} %cholesky.930), custom_call_target="Cholesky" | custom-call | tf_op jit(solution)/shard_map/jit(cholesky)/cholesky | solution.py:53
  167.7 10.0 custom-call.65
  181.1 11.7 %cholesky.716 = f32[128,128]{1,0:T(8,128)S(1)} custom-call(f32[128,128]{1,0:T(8,128)S(1)} %cholesky.935), custom_call_target="Cholesky" | custom-call | tf_op jit(solution)/shard_map/jit(cholesky)/cholesky | solution.py:53
  206.9 12.1 %cholesky.735 = f32[128,128]{1,0:T(8,128)S(1)} custom-call(f32[128,128]{1,0:T(8,128)S(1)} %cholesky.940), custom_call_target="Cholesky" | custom-call | tf_op jit(solution)/shard_map/jit(cholesky)/cholesky | solution.py:53
  220.3 9.8 custom-call.67
  232.7 11.7 %cholesky.752 = f32[128,128]{1,0:T(8,128)S(1)} custom-call(f32[128,128]{1,0:T(8,128)S(1)} %slice_subtract_fusion.13), custom_call_target="Cholesky" | custom-call | tf_op jit(solution)/shard_map/jit(cholesky)/cholesky | solution.py:53
  256.3 22.8 %while.2 = (s32[]{:T(128)}, f32[1024,1024]{1,0:T(8,128)}, s32[8,2]{0,1:T(2,128)S(1)}, f32[8,128,128]{2,1,0:T(8,128)S(1)}, s32[]{:T(128)}) while((s32[]{:T(128)}, f32[1024,1024]{1,0:T(8,128)}, s32[8,2]{0,1:T(2,128)S(1)}, f32[8,128,128]{2,1,0:T(8,128)S(1)}, s32[]{:T(128)}) %tuple.122), condition=%wide.while_cond, body=%wide.while_body.sunk | while | flops 2 | bytes 131181 | solution.py:44
  279.1 78.8 %custom-call.52 = f32[8,128,128]{1,2,0:T(8,128)S(1)} custom-call(f32[8,128,128]{2,1,0:T(8,128)S(1)} %get-tuple-element.10), custom_call_target="InvertDiagBlocksLowerTriangular" | custom-call | tf_op jit(solution)/shard_map/jit(_solve_triangular)/triangular_solve | solution.py:44
  404.0 10.0 subtract_convert_fusion
  419.8 23.5 %collective-permute-done.2 = bf16[512,1024]{0,1:T(8,128)(2,1)S(1)} collective-permute-done((bf16[512,1024]{0,1:T(8,128)(2,1)S(1)}, bf16[512,1024]{0,1:T(8,128)(2,1)S(1)}, u32[]{:S(2)}, u32[]{:S(2)}) %collective-permute-start.2) | collective-permute-done | bytes 1048608 | tf_op jit(solution)/shard_map/ppermute | solution.py:14
  475.4 11.7 %cholesky.767 = f32[128,128]{1,0:T(8,128)S(1)} custom-call(f32[128,128]{1,0:T(8,128)S(1)} %cholesky.944), custom_call_target="Cholesky" | custom-call | tf_op jit(solution)/shard_map/jit(cholesky)/cholesky | solution.py:78
  489.6 9.8 custom-call.68
  504.2 11.9 %cholesky.786 = f32[128,128]{1,0:T(8,128)S(1)} custom-call(f32[128,128]{1,0:T(8,128)S(1)} %cholesky.948), custom_call_target="Cholesky" | custom-call | tf_op jit(solution)/shard_map/jit(cholesky)/cholesky | solution.py:78
  518.1 9.8 custom-call.69
  532.9 13.2 %cholesky.807 = f32[128,128]{1,0:T(8,128)} custom-call(f32[128,128]{1,0:T(8,128)} %cholesky.953), custom_call_target="Cholesky" | custom-call | tf_op jit(solution)/shard_map/jit(cholesky)/cholesky | solution.py:78
  548.2 11.3 %custom-call.70 = f32[1,128,128]{1,2,0:T(8,128)} custom-call(f32[1,128,128]{2,1,0:T(8,128)} %get-tuple-element.105), custom_call_target="InvertDiagBlocksLowerTriangular" | custom-call | tf_op jit(solution)/shard_map/jit(cholesky)/cholesky | solution.py:78
  563.8 12.7 %cholesky.826 = f32[128,128]{1,0:T(8,128)} custom-call(f32[128,128]{1,0:T(8,128)S(1)} %cholesky.958), custom_call_target="Cholesky" | custom-call | tf_op jit(solution)/shard_map/jit(cholesky)/cholesky | solution.py:78
  578.6 10.4 %custom-call.71 = f32[1,128,128]{1,2,0:T(8,128)} custom-call(f32[1,128,128]{2,1,0:T(8,128)S(1)} %get-tuple-element.102), custom_call_target="InvertDiagBlocksLowerTriangular" | custom-call | tf_op jit(solution)/shard_map/jit(cholesky)/cholesky | solution.py:78
  593.4 11.7 %cholesky.845 = f32[128,128]{1,0:T(8,128)S(1)} custom-call(f32[128,128]{1,0:T(8,128)S(1)} %cholesky.963), custom_call_target="Cholesky" | custom-call | tf_op jit(solution)/shard_map/jit(cholesky)/cholesky | solution.py:78
  606.4 10.0 custom-call.72
  619.6 11.7 %cholesky.864 = f32[128,128]{1,0:T(8,128)S(1)} custom-call(f32[128,128]{1,0:T(8,128)S(1)} %cholesky.968), custom_call_target="Cholesky" | custom-call | tf_op jit(solution)/shard_map/jit(cholesky)/cholesky | solution.py:78
  645.4 11.9 %cholesky.883 = f32[128,128]{1,0:T(8,128)S(1)} custom-call(f32[128,128]{1,0:T(8,128)S(1)} %cholesky.973), custom_call_target="Cholesky" | custom-call | tf_op jit(solution)/shard_map/jit(cholesky)/cholesky | solution.py:78
  671.1 11.7 %cholesky.900 = f32[128,128]{1,0:T(8,128)S(1)} custom-call(f32[128,128]{1,0:T(8,128)S(1)} %slice_subtract_fusion.12), custom_call_target="Cholesky" | custom-call | tf_op jit(solution)/shard_map/jit(cholesky)/cholesky | solution.py:78
  694.6 28.1 %while.3 = (s32[]{:T(128)}, f32[1024,1024]{1,0:T(8,128)}, s32[8,2]{0,1:T(2,128)S(1)}, f32[8,128,128]{2,1,0:T(8,128)}, s32[]{:T(128)}) while((s32[]{:T(128)}, f32[1024,1024]{1,0:T(8,128)}, s32[8,2]{0,1:T(2,128)S(1)}, f32[8,128,128]{2,1,0:T(8,128)}, s32[]{:T(128)}) %tuple.130), condition=%wide.while_cond.1, body=%wide.while_body.1.sunk | while | flops 2 | bytes 132705 | solution.py:44
  722.7 80.4 %custom-call.53 = f32[8,128,128]{1,2,0:T(8,128)} custom-call(f32[8,128,128]{2,1,0:T(8,128)} %get-tuple-element.18), custom_call_target="InvertDiagBlocksLowerTriangular" | custom-call | tf_op jit(solution)/shard_map/jit(_solve_triangular)/triangular_solve | solution.py:44
  879.8 121.1 %all-reduce.9.cloned.1.call-done = f32[512,512]{1,0:T(8,128)} async-done(((f32[512,512]{1,0:T(8,128)}), f32[512,512]{1,0:T(8,128)}) %all-reduce.9.cloned.1.call-update) | async-done | bytes 1048592 | tf_op jit(solution)/shard_map/psum | solution.py:139
  (270 shorter events, 395.7 us)
Async XLA Ops:
  7.2 993.7 %all-reduce.9.cloned.1.call-start = ((), (), s32[]{:S(2)}) async-start(), calls=%async_computation | async-start | bytes 2097152 | tf_op jit(solution)/shard_map/psum | solution.py:139
  27.5 4.4 collective-permute-start
  45.9 1.9 copy-start.1
  399.6 4.4 collective-permute-start.1
  417.8 27.0 %copy-start.2 = (bf16[1,512,512]{2,1,0:T(8,128)(2,1)S(1)}, bf16[1,512,512]{2,1,0:T(8,128)(2,1)}, u32[]{:S(2)}) copy-start(bf16[1,512,512]{2,1,0:T(8,128)(2,1)} %param.14) | copy-start | bytes 1572868
  417.8 27.0 %copy-start.3 = (bf16[1,512,512]{2,1,0:T(8,128)(2,1)S(1)}, bf16[1,512,512]{2,1,0:T(8,128)(2,1)}, u32[]{:S(2)}) copy-start(bf16[1,512,512]{2,1,0:T(8,128)(2,1)} %param.13) | copy-start | bytes 1572868
  417.8 25.4 %collective-permute-start.2 = (bf16[512,1024]{0,1:T(8,128)(2,1)S(1)}, bf16[512,1024]{0,1:T(8,128)(2,1)S(1)}, u32[]{:S(2)}, u32[]{:S(2)}) collective-permute-start(bf16[512,1024]{0,1:T(8,128)(2,1)S(1)} %get-tuple-element.53), channel_id=1, source_target_pairs={{0,16},{16,0},{8,24},{24,8},{32,48},{48,32},{40,56},{56,40},{64,80... | collective-permute-start | bytes 3145736 | tf_op jit(solution)/shard_map/ppermute | solution.py:14
  444.8 12.1 %collective-permute-start.3 = (f32[512,1024]{0,1:T(8,128)}, f32[512,1024]{0,1:T(8,128)}, u32[]{:S(2)}, u32[]{:S(2)}) collective-permute-start(f32[512,1024]{0,1:T(8,128)} %convert_add_fusion.1), channel_id=1, source_target_pairs={{0,8},{8,0},{16,24},{24,16},{32,40},{40,32},{48,56},{56,48},{64,72... | collective-permute-start | bytes 6291464 | tf_op jit(solution)/shard_map/ppermute | solution.py:14
  445.5 423.3 %collective-permute-start.6 = (bf16[2,1,1,512]{3,2,1,0:T(2,128)(2,1)}, bf16[2,1,1,512]{3,2,1,0:T(2,128)(2,1)S(1)}, u32[]{:S(2)}, u32[]{:S(2)}) collective-permute-start(bf16[2,1,1,512]{3,2,1,0:T(2,128)(2,1)} %get-tuple-element.54), channel_id=1, source_target_pairs={{0,8},{8,16},{16,24},{24,32},{32,40},{40,48},{48,56},{56,64},{64,7... | collective-permute-start | bytes 6152 | tf_op jit(solution)/shard_map/ppermute | solution.py:22
  447.9 420.9 %collective-permute-start.7 = (bf16[2,1,1,512]{3,2,1,0:T(2,128)(2,1)S(1)}, bf16[2,1,1,512]{3,2,1,0:T(2,128)(2,1)}, u32[]{:S(2)}, u32[]{:S(2)}) collective-permute-start(bf16[2,1,1,512]{3,2,1,0:T(2,128)(2,1)S(1)} %get-tuple-element.55), channel_id=1, source_target_pairs={{8,0},{16,8},{24,16},{32,24},{40,32},{48,40},{56,48},{64,56},{72,6... | collective-permute-start | bytes 6152 | tf_op jit(solution)/shard_map/ppermute | solution.py:25
  454.4 1.5 copy-start.12
  473.4 1.9 copy-start
  503.3 0.8 copy-start.9
  808.9 7.8 copy-start.6
  812.6 4.0 copy-start.8
  816.7 0.7 copy-start.10
  834.5 26.0 %copy-start.13 = (s32[1,256,1]{1,2,0:T(1,128)S(1)}, s32[1,256,1]{1,2,0:T(1,128)}, u32[]{:S(2)}) copy-start(s32[1,256,1]{1,2,0:T(1,128)} %fusion.242) | copy-start | bytes 3076
  856.6 13.3 %collective-permute-start.4 = (bf16[1024,512]{0,1:T(8,128)(2,1)}, bf16[1024,512]{0,1:T(8,128)(2,1)}, u32[]{:S(2)}, u32[]{:S(2)}) collective-permute-start(bf16[1024,512]{0,1:T(8,128)(2,1)} %fusion.48), channel_id=1, source_target_pairs={{0,8},{8,0},{16,24},{24,16},{32,40},{40,32},{48,56},{56,48},{64,72... | collective-permute-start | bytes 3145736 | tf_op jit(solution)/shard_map/ppermute | solution.py:14
  868.8 5.7 copy-start.4
  874.5 3.6 copy-start.5
  874.5 3.6 copy-start.11
  874.5 129.3 %collective-permute-start.5 = (bf16[1024,1024]{0,1:T(8,128)(2,1)}, bf16[1024,1024]{0,1:T(8,128)(2,1)}, u32[]{:S(2)}, u32[]{:S(2)}) collective-permute-start(bf16[1024,1024]{0,1:T(8,128)(2,1)} %maximum_select_fusion.11), channel_id=1, source_target_pairs={{0,16},{16,0},{8,24},{24,8},{32,48},{48,32},{40,56},{56,40},{64,80... | collective-permute-start | bytes 6291464 | tf_op jit(solution)/shard_map/ppermute | solution.py:14
  878.1 124.4 %copy-start.7 = (bf16[1024,512]{0,1:T(8,128)(2,1)S(1)}, bf16[1024,512]{0,1:T(8,128)(2,1)}, u32[]{:S(2)}) copy-start(bf16[1024,512]{0,1:T(8,128)(2,1)} %get-tuple-element.49) | copy-start | bytes 3145732
Sparse Core Ops, SparseCore 0:
  879.9 120.9 all-reduce.8
where the time goes:
time: 1030 us; the launch traced here: 1020 us
  other arithmetic  572 us (56%)
  waiting for transfers between devices  153 us (15%)
  matrix products  133 us (13%)
  local copies, waits for them, and re-layouts  125 us (12%)
  between operations  25.5 us (2%)
  starting transfers between devices  10.4 us (1%)
    another operation x31, other arithmetic, level_two(): factor = jnp.linalg.cholesky(schur)  179 us
    another operation x30, other arithmetic, level_one(): factor = jnp.linalg.cholesky(schur)  173 us
    another operation x5, other arithmetic, triangular(): return jax.scipy.linalg.solve_triangular(factor, right_side, lower=True)  169 us
    psum x1, waiting for transfers between devices, body(): total = lax.psum(gradient_term, 'freq')  121 us
    another operation x30, matrix products, triangular(): return jax.scipy.linalg.solve_triangular(factor, right_side, lower=True)  67.7 us
    another operation x48, local copies, waits for them, and re-layouts  50.8 us
    unnamed x48, local copies, waits for them, and re-layouts  37.5 us
    ppermute x6, waiting for transfers between devices, from_partner(): return lax.ppermute(block, axis, route)  32.1 us
  transfers between devices with their start and end apart: 9, of which 4 were waited for; matrix products, arithmetic and copies ran while one was open for 41% of the time, Pallas kernels for 0%

commit v1 on v0

--- a/solution.py
+++ b/solution.py
@@ -136,7 +136,7 @@
         kappa_sq * (state_full * state_residual + adjoint_full * adjoint_residual), axis=0
     )
     share_rows = gradient_term.shape[0] // lax.axis_size("freq")
-    total = lax.psum(gradient_term, "freq")
+    total = jnp.sum(lax.all_gather(gradient_term, "freq"), axis=0)
     medium_gradient = lax.dynamic_slice_in_dim(
         total, lax.axis_index("freq") * share_rows, share_rows, 0
     )

time: 1030 us -> 914 us (0.89)
  waiting for transfers between devices: 153 us -> 70.7 us
  local copies, waits for them, and re-layouts: 125 us -> 105 us
    psum x1 -> x0, waiting for transfers between devices: 121 us -> none  [body(): total = lax.psum(gradient_term, 'freq')]
    ppermute x6, waiting for transfers between devices: 32.1 us -> 70.6 us  [from_partner(): return lax.ppermute(block, axis, route)]
  transfers between devices with their start and end apart: 9 -> 9, of which waited for: 4 -> 5; matrix products, arithmetic and copies ran while one was open for 41% -> 43% of each run, Pallas kernels for 0% -> 0%
where the time goes in v1:
time: 914 us; the launch traced here: 906 us
  other arithmetic  563 us (62%)
  matrix products  128 us (14%)
  local copies, waits for them, and re-layouts  105 us (11%)
  waiting for transfers between devices  70.7 us (8%)
  between operations  25.4 us (3%)
  starting transfers between devices  13.3 us (1%)
    another operation x30, other arithmetic, level_one(): factor = jnp.linalg.cholesky(schur)  173 us
    another operation x31, other arithmetic, level_two(): factor = jnp.linalg.cholesky(schur)  173 us
    another operation x5, other arithmetic, triangular(): return jax.scipy.linalg.solve_triangular(factor, right_side, lower=True)  168 us
    ppermute x6, waiting for transfers between devices, from_partner(): return lax.ppermute(block, axis, route)  70.6 us
    another operation x30, matrix products, triangular(): return jax.scipy.linalg.solve_triangular(factor, right_side, lower=True)  65.4 us
    another operation x48, local copies, waits for them, and re-layouts  46.1 us
    unnamed x48, local copies, waits for them, and re-layouts  29.7 us
    another operation x14, matrix products, level_two(): factor = jnp.linalg.cholesky(schur)  23.1 us
  transfers between devices with their start and end apart: 9, of which 5 were waited for; matrix products, arithmetic and copies ran while one was open for 43% of the time, Pallas kernels for 0%

profile of v1, /device:TPU:8, one launch (start us, length us, event | category | flops | bytes accessed | tf_op | source)
XLA Modules:
  0.0 905.7 jit_solution(17914077031980390795)
XLA Ops:
  7.2 12.3 %copy.54 = bf16[1,2048,2048]{1,2,0:T(8,128)(2,1)} copy(bf16[1,2048,2048]{2,1,0:T(8,128)(2,1)} %param.9) | data formatting | bytes 16777216 | tf_op args[0]
  47.9 11.7 %cholesky.619 = f32[128,128]{1,0:T(8,128)S(1)} custom-call(f32[128,128]{1,0:T(8,128)S(1)} %cholesky.911), custom_call_target="Cholesky" | custom-call | tf_op jit(solution)/shard_map/jit(cholesky)/cholesky | solution.py:53
  59.6 9.8 %custom-call.61 = f32[1,128,128]{1,2,0:T(8,128)S(1)} custom-call(f32[1,128,128]{2,1,0:T(8,128)S(1)} %get-tuple-element.135), custom_call_target="InvertDiagBlocksLowerTriangular" | custom-call | tf_op jit(solution)/shard_map/jit(cholesky)/cholesky | solution.py:53
  75.9 12.2 %cholesky.638 = f32[128,128]{1,0:T(8,128)S(1)} custom-call(f32[128,128]{1,0:T(8,128)S(1)} %cholesky.915), custom_call_target="Cholesky" | custom-call | tf_op jit(solution)/shard_map/jit(cholesky)/cholesky | solution.py:53
  101.9 11.7 %cholesky.659 = f32[128,128]{1,0:T(8,128)S(1)} custom-call(f32[128,128]{1,0:T(8,128)S(1)} %cholesky.920), custom_call_target="Cholesky" | custom-call | tf_op jit(solution)/shard_map/jit(cholesky)/cholesky | solution.py:53
  128.2 11.9 %cholesky.678 = f32[128,128]{1,0:T(8,128)S(1)} custom-call(f32[128,128]{1,0:T(8,128)S(1)} %cholesky.925), custom_call_target="Cholesky" | custom-call | tf_op jit(solution)/shard_map/jit(cholesky)/cholesky | solution.py:53
  154.7 11.7 %cholesky.697 = f32[128,128]{1,0:T(8,128)S(1)} custom-call(f32[128,128]{1,0:T(8,128)S(1)} %cholesky.930), custom_call_target="Cholesky" | custom-call | tf_op jit(solution)/shard_map/jit(cholesky)/cholesky | solution.py:53
  167.7 10.0 %custom-call.65 = f32[1,128,128]{1,2,0:T(8,128)S(1)} custom-call(f32[1,128,128]{2,1,0:T(8,128)S(1)} %get-tuple-element.123), custom_call_target="InvertDiagBlocksLowerTriangular" | custom-call | tf_op jit(solution)/shard_map/jit(cholesky)/cholesky | solution.py:53
  181.1 11.7 %cholesky.716 = f32[128,128]{1,0:T(8,128)S(1)} custom-call(f32[128,128]{1,0:T(8,128)S(1)} %cholesky.935), custom_call_target="Cholesky" | custom-call | tf_op jit(solution)/shard_map/jit(cholesky)/cholesky | solution.py:53
  206.9 12.1 %cholesky.735 = f32[128,128]{1,0:T(8,128)S(1)} custom-call(f32[128,128]{1,0:T(8,128)S(1)} %cholesky.940), custom_call_target="Cholesky" | custom-call | tf_op jit(solution)/shard_map/jit(cholesky)/cholesky | solution.py:53
  220.3 9.8 %custom-call.67 = f32[1,128,128]{1,2,0:T(8,128)S(1)} custom-call(f32[1,128,128]{2,1,0:T(8,128)S(1)} %get-tuple-element.117), custom_call_target="InvertDiagBlocksLowerTriangular" | custom-call | tf_op jit(solution)/shard_map/jit(cholesky)/cholesky | solution.py:53
  232.7 11.7 %cholesky.752 = f32[128,128]{1,0:T(8,128)S(1)} custom-call(f32[128,128]{1,0:T(8,128)S(1)} %slice_subtract_fusion.13), custom_call_target="Cholesky" | custom-call | tf_op jit(solution)/shard_map/jit(cholesky)/cholesky | solution.py:53
  256.3 22.8 %while.2 = (s32[]{:T(128)}, f32[1024,1024]{1,0:T(8,128)}, s32[8,2]{0,1:T(2,128)S(1)}, f32[8,128,128]{2,1,0:T(8,128)S(1)}, s32[]{:T(128)}) while((s32[]{:T(128)}, f32[1024,1024]{1,0:T(8,128)}, s32[8,2]{0,1:T(2,128)S(1)}, f32[8,128,128]{2,1,0:T(8,128)S(1)}, s32[]{:T(128)}) %tuple.123), condition=%wide.while_cond, body=%wide.while_body.sunk | while | flops 2 | bytes 131181 | solution.py:44
  279.1 78.8 %custom-call.52 = f32[8,128,128]{1,2,0:T(8,128)S(1)} custom-call(f32[8,128,128]{2,1,0:T(8,128)S(1)} %get-tuple-element.10), custom_call_target="InvertDiagBlocksLowerTriangular" | custom-call | tf_op jit(solution)/shard_map/jit(_solve_triangular)/triangular_solve | solution.py:44
  404.0 10.0 %subtract_convert_fusion = bf16[1024,2048]{0,1:T(8,128)(2,1)S(1)} fusion(f32[1024,1024]{0,1:T(8,128)} %get-tuple-element.50, pred[]{:T(512)S(6)} %eq.5, bf16[1024,1024]{0,1:T(8,128)(2,1)} %fusion.47, bf16[1024,1024]{0,1:T(8,128)(2,1)S(1)} %collective-permute-done.1), kind=kOutput, calls=%fused_computation.6 | convolution fusion | flops 4320133120 | bytes 12582913 | tf_op jit(solution)/shard_map/dot_general | solution.py:57
  428.3 14.9 %collective-permute-done.2 = bf16[512,1024]{0,1:T(8,128)(2,1)S(1)} collective-permute-done((bf16[512,1024]{0,1:T(8,128)(2,1)S(1)}, bf16[512,1024]{0,1:T(8,128)(2,1)S(1)}, u32[]{:S(2)}, u32[]{:S(2)}) %collective-permute-start.2) | collective-permute-done | bytes 1048608 | tf_op jit(solution)/shard_map/ppermute | solution.py:14
  483.3 11.7 %cholesky.767 = f32[128,128]{1,0:T(8,128)S(1)} custom-call(f32[128,128]{1,0:T(8,128)S(1)} %cholesky.944), custom_call_target="Cholesky" | custom-call | tf_op jit(solution)/shard_map/jit(cholesky)/cholesky | solution.py:78
  497.5 9.8 %custom-call.68 = f32[1,128,128]{1,2,0:T(8,128)S(1)} custom-call(f32[1,128,128]{2,1,0:T(8,128)S(1)} %get-tuple-element.113), custom_call_target="InvertDiagBlocksLowerTriangular" | custom-call | tf_op jit(solution)/shard_map/jit(cholesky)/cholesky | solution.py:78
  511.3 11.9 %cholesky.786 = f32[128,128]{1,0:T(8,128)S(1)} custom-call(f32[128,128]{1,0:T(8,128)S(1)} %cholesky.948), custom_call_target="Cholesky" | custom-call | tf_op jit(solution)/shard_map/jit(cholesky)/cholesky | solution.py:78
  523.8 9.8 %custom-call.69 = f32[1,128,128]{1,2,0:T(8,128)S(1)} custom-call(f32[1,128,128]{2,1,0:T(8,128)S(1)} %get-tuple-element.110), custom_call_target="InvertDiagBlocksLowerTriangular" | custom-call | tf_op jit(solution)/shard_map/jit(cholesky)/cholesky | solution.py:78
  537.0 11.7 %cholesky.807 = f32[128,128]{1,0:T(8,128)S(1)} custom-call(f32[128,128]{1,0:T(8,128)S(1)} %cholesky.953), custom_call_target="Cholesky" | custom-call | tf_op jit(solution)/shard_map/jit(cholesky)/cholesky | solution.py:78
  562.7 12.1 %cholesky.826 = f32[128,128]{1,0:T(8,128)S(1)} custom-call(f32[128,128]{1,0:T(8,128)S(1)} %cholesky.958), custom_call_target="Cholesky" | custom-call | tf_op jit(solution)/shard_map/jit(cholesky)/cholesky | solution.py:78
  575.5 9.8 %custom-call.71 = f32[1,128,128]{1,2,0:T(8,128)S(1)} custom-call(f32[1,128,128]{2,1,0:T(8,128)S(1)} %get-tuple-element.104), custom_call_target="InvertDiagBlocksLowerTriangular" | custom-call | tf_op jit(solution)/shard_map/jit(cholesky)/cholesky | solution.py:78
  588.7 11.7 %cholesky.845 = f32[128,128]{1,0:T(8,128)S(1)} custom-call(f32[128,128]{1,0:T(8,128)S(1)} %cholesky.963), custom_call_target="Cholesky" | custom-call | tf_op jit(solution)/shard_map/jit(cholesky)/cholesky | solution.py:78
  601.1 10.0 %custom-call.72 = f32[1,128,128]{1,2,0:T(8,128)S(1)} custom-call(f32[1,128,128]{2,1,0:T(8,128)S(1)} %get-tuple-element.101), custom_call_target="InvertDiagBlocksLowerTriangular" | custom-call | tf_op jit(solution)/shard_map/jit(cholesky)/cholesky | solution.py:78
  614.4 11.7 %cholesky.864 = f32[128,128]{1,0:T(8,128)S(1)} custom-call(f32[128,128]{1,0:T(8,128)S(1)} %cholesky.968), custom_call_target="Cholesky" | custom-call | tf_op jit(solution)/shard_map/jit(cholesky)/cholesky | solution.py:78
  626.7 9.8 %custom-call.73 = f32[1,128,128]{1,2,0:T(8,128)S(1)} custom-call(f32[1,128,128]{2,1,0:T(8,128)S(1)} %get-tuple-element.98), custom_call_target="InvertDiagBlocksLowerTriangular" | custom-call | tf_op jit(solution)/shard_map/jit(cholesky)/cholesky | solution.py:78
  639.5 11.7 %cholesky.883 = f32[128,128]{1,0:T(8,128)S(1)} custom-call(f32[128,128]{1,0:T(8,128)S(1)} %cholesky.973), custom_call_target="Cholesky" | custom-call | tf_op jit(solution)/shard_map/jit(cholesky)/cholesky | solution.py:78
  664.3 11.7 %cholesky.900 = f32[128,128]{1,0:T(8,128)S(1)} custom-call(f32[128,128]{1,0:T(8,128)S(1)} %slice_subtract_fusion.12), custom_call_target="Cholesky" | custom-call | tf_op jit(solution)/shard_map/jit(cholesky)/cholesky | solution.py:78
  691.5 23.6 %while.3 = (s32[]{:T(128)}, f32[1024,1024]{1,0:T(8,128)}, s32[8,2]{0,1:T(2,128)S(1)}, f32[8,128,128]{2,1,0:T(8,128)S(1)}, s32[]{:T(128)}) while((s32[]{:T(128)}, f32[1024,1024]{1,0:T(8,128)}, s32[8,2]{0,1:T(2,128)S(1)}, f32[8,128,128]{2,1,0:T(8,128)S(1)}, s32[]{:T(128)}) %tuple.131), condition=%wide.while_cond.1, body=%wide.while_body.1.sunk | while | flops 2 | bytes 131181 | solution.py:44
  715.1 79.0 %custom-call.53 = f32[8,128,128]{1,2,0:T(8,128)S(1)} custom-call(f32[8,128,128]{2,1,0:T(8,128)S(1)} %get-tuple-element.18), custom_call_target="InvertDiagBlocksLowerTriangular" | custom-call | tf_op jit(solution)/shard_map/jit(_solve_triangular)/triangular_solve | solution.py:44
  838.4 44.9 %collective-permute-done.5 = bf16[1024,1024]{0,1:T(8,128)(2,1)} collective-permute-done((bf16[1024,1024]{0,1:T(8,128)(2,1)S(1)}, bf16[1024,1024]{0,1:T(8,128)(2,1)}, u32[]{:S(2)}, u32[]{:S(2)}) %collective-permute-start.5) | collective-permute-done | bytes 2097184 | tf_op jit(solution)/shard_map/ppermute | solution.py:14
  (271 shorter events, 372.3 us)
Async XLA Ops:
  7.2 886.3 %all-gather.2.cloned.1.call-start = ((), (), s32[]{:S(2)}) async-start(), calls=%async_computation | async-start | bytes 9437184 | tf_op jit(solution)/shard_map/all_gather | solution.py:139
  27.5 4.4 collective-permute-start
  45.9 1.9 copy-start
  399.6 4.4 collective-permute-start.1
  415.8 4.0 copy-start.2
  415.8 4.0 copy-start.3
  415.8 12.4 %copy-start.12 = (s32[1,256]{1,0:T(1,128)S(1)}, s32[1,256]{1,0:T(1,128)}, u32[]{:S(2)}) copy-start(s32[1,256]{1,0:T(1,128)} %param.15) | copy-start | bytes 3076
  417.8 25.4 %collective-permute-start.2 = (bf16[512,1024]{0,1:T(8,128)(2,1)S(1)}, bf16[512,1024]{0,1:T(8,128)(2,1)S(1)}, u32[]{:S(2)}, u32[]{:S(2)}) collective-permute-start(bf16[512,1024]{0,1:T(8,128)(2,1)S(1)} %get-tuple-element.55), channel_id=1, source_target_pairs={{0,16},{16,0},{8,24},{24,8},{32,48},{48,32},{40,56},{56,40},{64,80... | collective-permute-start | bytes 3145736 | tf_op jit(solution)/shard_map/ppermute | solution.py:14
  419.8 37.9 %collective-permute-start.6 = (bf16[2,1,1,512]{3,2,1,0:T(2,128)(2,1)S(1)}, bf16[2,1,1,512]{3,2,1,0:T(2,128)(2,1)S(1)}, u32[]{:S(2)}, u32[]{:S(2)}) collective-permute-start(bf16[2,1,1,512]{3,2,1,0:T(2,128)(2,1)S(1)} %get-tuple-element.56), channel_id=1, source_target_pairs={{0,8},{8,16},{16,24},{24,32},{32,40},{40,48},{48,56},{56,64},{64,7... | collective-permute-start | bytes 6152 | tf_op jit(solution)/shard_map/ppermute | solution.py:22
  421.7 36.0 %collective-permute-start.7 = (bf16[2,1,1,512]{3,2,1,0:T(2,128)(2,1)S(1)}, bf16[2,1,1,512]{3,2,1,0:T(2,128)(2,1)S(1)}, u32[]{:S(2)}, u32[]{:S(2)}) collective-permute-start(bf16[2,1,1,512]{3,2,1,0:T(2,128)(2,1)S(1)} %get-tuple-element.57), channel_id=1, source_target_pairs={{8,0},{16,8},{24,16},{32,24},{40,32},{48,40},{56,48},{64,56},{72,6... | collective-permute-start | bytes 6152 | tf_op jit(solution)/shard_map/ppermute | solution.py:25
  428.3 21.8 %copy-start.13 = (bf16[1,256]{1,0:T(2,128)(2,1)S(1)}, bf16[1,256]{1,0:T(2,128)(2,1)}, u32[]{:S(2)}) copy-start(bf16[1,256]{1,0:T(2,128)(2,1)} %param.16) | copy-start | bytes 1540
  444.9 19.6 %collective-permute-start.3 = (f32[512,1024]{0,1:T(8,128)}, f32[512,1024]{0,1:T(8,128)}, u32[]{:S(2)}, u32[]{:S(2)}) collective-permute-start(f32[512,1024]{0,1:T(8,128)} %convert_add_fusion.1), channel_id=1, source_target_pairs={{0,8},{8,0},{16,24},{24,16},{32,40},{40,32},{48,56},{56,48},{64,72... | collective-permute-start | bytes 6291464 | tf_op jit(solution)/shard_map/ppermute | solution.py:14
  458.0 4.8 copy-start.5
  458.0 4.8 copy-start.10
  481.3 2.0 copy-start.1
  686.4 110.0 %copy-start.4 = (f32[1024,512]{1,0:T(8,128)S(1)}, f32[1024,512]{1,0:T(8,128)}, u32[]{:S(2)}) copy-start(f32[1024,512]{1,0:T(8,128)} %get-tuple-element.41) | copy-start | bytes 6291460
  794.1 2.3 copy-start.11
  812.1 11.3 %copy-start.9 = (bf16[128,512]{0,1:T(8,128)(2,1)S(1)}, bf16[128,512]{0,1:T(8,128)(2,1)}, u32[]{:S(2)}) copy-start(bf16[128,512]{0,1:T(8,128)(2,1)} %copy.69) | copy-start | bytes 393220
  823.4 13.5 %copy-start.6 = (bf16[1024,512]{0,1:T(8,128)(2,1)S(1)}, bf16[1024,512]{0,1:T(8,128)(2,1)}, u32[]{:S(2)}) copy-start(bf16[1024,512]{0,1:T(8,128)(2,1)} %get-tuple-element.51) | copy-start | bytes 3145732
  830.7 3.0 copy-start.7
  830.8 3.0 collective-permute-start.4
  834.8 48.4 %collective-permute-start.5 = (bf16[1024,1024]{0,1:T(8,128)(2,1)S(1)}, bf16[1024,1024]{0,1:T(8,128)(2,1)}, u32[]{:S(2)}, u32[]{:S(2)}) collective-permute-start(bf16[1024,1024]{0,1:T(8,128)(2,1)S(1)} %maximum_select_fusion.11), channel_id=1, source_target_pairs={{0,16},{16,0},{8,24},{24,8},{32,48},{48,32},{40,56},{56,40},{64,80... | collective-permute-start | bytes 6291464 | tf_op jit(solution)/shard_map/ppermute | solution.py:14
  837.0 46.3 %copy-start.8 = (bf16[1024,512]{0,1:T(8,128)(2,1)S(1)}, bf16[1024,512]{0,1:T(8,128)(2,1)}, u32[]{:S(2)}) copy-start(bf16[1024,512]{0,1:T(8,128)(2,1)} %copy-done.7) | copy-start | bytes 3145732
Sparse Core Ops, SparseCore 0:
  464.6 176.2 all-gather.1
